TPU v7x, 32 devices: a whole 2x2x4 slice. The times are simulated.
32 devices in a mesh: row: 2 (over y), col: 4 (over x, core), pair: 4 (over z).
Axes of the slice: x: 2, y: 2, z: 4, core: 2. Of those that a mesh axis runs over, the one named last changes fastest.
Arguments:
- amps: bfloat16 [512, 512, 512], P('pair', 'row', 'col'), may hold values from -6 to 6
- integrals: bfloat16 [4096, 512, 512], P('pair', 'row', 'col'), may hold values from -0.01171875 to 0.01171875
- mask_amps: int32 [8, 8], replicated, may hold values 0 or 1
- mask_ints: int32 [8, 8], replicated, may hold values 0 or 1
Outputs:
- residual: bfloat16 [512, 4096], P(('row', 'col'), 'pair')
All inputs are finite; a program needn't handle non-finite values.
Results may differ from a plain program's by a relative error of at most 0.00115.
Values may be sent and summed in bfloat16 or wider, within the bound.
No kernel may reach another device: no remote copies, remote signals or barrier semaphores. Data moves between devices by JAX's collectives and lax.ppermute only.
A program may use at most 192 MiB of HBM per device.

v0:
```python
import functools

import jax
import jax.numpy as jnp
from jax import lax
from jax.experimental import pallas as pl
from jax.experimental.pallas import tpu as pltpu
from jax.sharding import PartitionSpec as P

TILE = 64
WIN = 64
LANES = 128
AB_BLOCK = 512
PIECE = 4
VMEM_LIMIT = 50 * 1024 * 1024

LAST, LONG, CORE, LENT, UNITS = 0, 1, 2, 3, 8
HEAD, SECOND, THIRD, RARE = 0, 1, 2, 3


class Sizes:
    def __init__(self, amps, integrals):
        self.pairs, self.local_c, self.local_d = amps.shape
        self.local_ab = integrals.shape[0]
        self.uc = min(self.local_c, TILE)
        self.ud = min(self.local_d, TILE)
        self.nud = self.local_d // self.ud
        self.units = (self.local_c // self.uc) * self.nud
        self.half = self.pairs // 2
        self.rows = self.uc // 2
        self.k = self.rows * LANES
        self.most = 2 * self.units
        self.long = self.most > PIECE
        self.places = (4 if self.long else 1) * PIECE
        self.slot_mine = UNITS + self.units
        self.slot_other = self.slot_mine + self.places
        self.table = self.slot_other + self.places


def lending(counts, here, there):
    move = jnp.minimum((here - there) // 2, 2)
    richer = jnp.where(counts[0] >= counts[1], 0, 1)
    return [jnp.where((counts[c] > 0) & ((move == 2) | ((move == 1) & (richer == c))), 1, 0) for c in range(2)]


def plan_kernel(z, rows, cols, pos_ref, ma_ref, mi_ref, table_ref):
    row, col = pos_ref[0], pos_ref[1]
    core, chip = lax.rem(col, 2), col // 2

    def active(r, c, unit):
        ct = (r * z.local_c + (unit // z.nud) * z.uc) // TILE
        dt = (c * z.local_d + lax.rem(unit, z.nud) * z.ud) // TILE
        return jnp.where(ma_ref[ct, dt] * mi_ref[ct, dt] != 0, 1, 0)

    def count(r, c):
        return lax.fori_loop(0, z.units, lambda u, n: n + active(r, c, u), 0)

    table_ref[CORE] = core
    for i in range(z.units):
        table_ref[UNITS + i] = 0

    def fill(u, n):
        on = active(row, col, u)

        @pl.when(on == 1)
        def _():
            table_ref[UNITS + n] = u

        return n + on

    own = lax.fori_loop(0, z.units, fill, 0)
    zero = jnp.int32(0)
    if z.long:
        grid = [(r, x) for r in range(2) for x in range(2)]
        n = {g: [count(g[0], 2 * g[1] + c) for c in range(2)] for g in grid}
        all_n = {g: n[g][0] + n[g][1] for g in grid}
        lent_x = {(r, x): lending(n[r, x], all_n[r, x], all_n[r, 1 - x]) for r, x in grid}
        n = {g: [n[g][c] - lent_x[g][c] for c in range(2)] for g in grid}
        all_n = {(r, x): sum(n[r, x]) + sum(lent_x[r, 1 - x]) for r, x in grid}
        lent_y = {(r, x): lending(n[r, x], all_n[r, x], all_n[1 - r, x]) for r, x in grid}
        n = {g: [n[g][c] - lent_y[g][c] for c in range(2)] for g in grid}
        all_n = {(r, x): sum(n[r, x]) + sum(lent_x[r, 1 - x]) + sum(lent_y[1 - r, x]) for r, x in grid}
        slots = jnp.int32(1)
        for g in grid:
            slots = jnp.maximum(slots, all_n[g])

        def here(get):
            upper = jnp.where(chip == 0, get(0, 0), get(0, 1))
            return jnp.where(row == 0, upper, jnp.where(chip == 0, get(1, 0), get(1, 1)))

        kept = [here(lambda r, x: n[r, x][c]) for c in range(2)]
        gives = [here(lambda r, x: jnp.where(core == 0, v[r, x][0], v[r, x][1])) for v in (lent_x, lent_y)]
        got = [here(lambda r, x: lent_x[r, 1 - x][c]) for c in range(2)]
        got += [here(lambda r, x: lent_y[1 - r, x][c]) for c in range(2)]
        is_long = slots > 3 * PIECE
        last_len = jnp.maximum(slots - jnp.where(is_long, 3, 2) * PIECE, 0)
    else:

        def most(g, n):
            r, x = g // (cols // 2), lax.rem(g, cols // 2)
            return jnp.maximum(n, count(r, 2 * x) + count(r, 2 * x + 1))

        slots = lax.fori_loop(0, rows * (cols // 2), most, 1)
        other = count(row, col + 1 - 2 * core)
        kept = [jnp.where(core == 0, own, other), jnp.where(core == 0, other, own)]
        gives, got = [zero, zero], [zero] * 4
        is_long, last_len = slots > PIECE, slots
    table_ref[LAST] = last_len
    table_ref[LONG] = jnp.where(is_long, 1, 0)
    for d in range(2):
        at = own - 1 - (gives[0] if d else 0)
        table_ref[LENT + d] = jnp.where(gives[d] == 1, table_ref[UNITS + jnp.clip(at, 0, z.units - 1)], -1)

    first, second = kept
    extra = jnp.abs(first - second)
    richer = jnp.where(first >= second, 0, 1)
    for at in range(z.places):
        piece, j = divmod(at, PIECE)
        borrowed = jnp.bool_(False)
        s = zero + at
        if piece == SECOND:
            borrowed = got[j] == 1
            s = s - sum(got[:j], zero)
        elif piece == THIRD:
            s = s - sum(got, zero) + jnp.where(is_long, PIECE, 0)
        elif piece == RARE:
            s = s - sum(got, zero) - PIECE
        live = jnp.logical_not(borrowed) & (s < first + second)
        if piece == RARE:
            live &= is_long
        k = s - extra
        owner = jnp.where(s < extra, richer, lax.rem(jnp.maximum(k, 0), 2))
        index = jnp.where(s < extra, s, k // 2 + jnp.where(owner == richer, extra, 0))
        unit = table_ref[UNITS + jnp.clip(index, 0, z.units - 1)]
        mine = jnp.where(live & (owner == core), unit, -1)
        theirs = live & (owner != core)
        if piece == SECOND:
            mine = jnp.where(borrowed & (core == j % 2), z.units + j // 2, mine)
            theirs |= borrowed & (core != j % 2)
        table_ref[z.slot_mine + at] = mine
        table_ref[z.slot_other + at] = jnp.where(theirs, 1, 0)


def make_plan(z, mask_amps, mask_ints):
    rows, cols = lax.axis_size("row"), lax.axis_size("col")
    pos = jnp.stack([lax.axis_index("row"), lax.axis_index("col")]).astype(jnp.int32)
    smem = pl.BlockSpec(memory_space=pltpu.SMEM)
    return pl.pallas_call(
        functools.partial(plan_kernel, z, rows, cols),
        out_shape=jax.ShapeDtypeStruct((z.table,), jnp.int32),
        in_specs=[smem] * 3,
        out_specs=smem,
        name="plan",
    )(pos, mask_amps, mask_ints)


def squeeze_tile(second, x, y):
    low = lax.broadcasted_iota(jnp.int32, x.shape, 2) < TILE
    if second:
        return jnp.where(low, jnp.concatenate([x[..., TILE:], x[..., :TILE]], -1), y)
    return jnp.where(low, x, jnp.concatenate([y[..., TILE:], y[..., :TILE]], -1))


def pack_tile(z, unit, on, a_ref, o_ref):
    for second in range(z.nud):

        @pl.when(on & (lax.rem(unit, z.nud) == second))
        def _(second=second):
            v = squeeze_tile(second, a_ref[:, : z.rows, :], a_ref[:, z.rows :, :])
            o_ref[0] = v.reshape(z.half, z.k)


def pack_slots(z, table, amps, start, count, kept, borrowed=(), received=None):
    def unit_of(t, i):
        return t[z.slot_mine + start + i]

    def other(t, i):
        return t[z.slot_other + start + i]

    def half(t):
        return t[CORE] if kept else 1 - t[CORE]

    def tile(t, i):
        unit = unit_of(t, i)
        return jnp.where((unit >= 0) & (unit < z.units), unit, 0) // z.nud

    def body(t, a_ref, *refs):
        o_ref = refs[-1]
        i = pl.program_id(0)
        unit = unit_of(t, i)
        pack_tile(z, unit, (unit >= 0) & (unit < z.units), a_ref, o_ref)
        for d in range(len(borrowed)):

            @pl.when(unit == z.units + d)
            def _(d=d):
                o_ref[0] = refs[d][0]

        if kept:

            @pl.when(other(t, i) == 1)
            def _():
                o_ref[0] = refs[-2][0]

    in_specs = [pl.BlockSpec((z.half, z.uc, LANES), lambda i, t: (half(t), tile(t, i), 0))]
    in_specs += [pl.BlockSpec((1, z.half, z.k), lambda i, t: (half(t), 0, 0))] * len(borrowed)
    args = [amps, *borrowed]
    if kept:
        in_specs.append(pl.BlockSpec((1, z.half, z.k), lambda i, t: (jnp.where(other(t, i) == 1, i, 0), 0, 0)))
        args.append(received)
    return pl.pallas_call(
        body,
        grid_spec=pltpu.PrefetchScalarGridSpec(
            num_scalar_prefetch=1,
            grid=(count,),
            in_specs=in_specs,
            out_specs=pl.BlockSpec((1, z.half, z.k), lambda i, t: (i, 0, 0)),
        ),
        out_shape=jax.ShapeDtypeStruct((count, z.half, z.k), jnp.bfloat16),
        compiler_params=pltpu.CompilerParams(vmem_limit_bytes=VMEM_LIMIT),
        cost_estimate=pl.CostEstimate(flops=0, bytes_accessed=4 * count * z.half * z.k * 2, transcendentals=0),
        name="pack_kept" if kept else "pack_given",
    )(table, *args)


def lend_amps(z, table, amps, way):
    def body(t, a_ref, o_ref):
        unit = t[LENT + way]
        pack_tile(z, unit, unit >= 0, a_ref, o_ref)

    return pl.pallas_call(
        body,
        grid_spec=pltpu.PrefetchScalarGridSpec(
            num_scalar_prefetch=1,
            grid=(2,),
            in_specs=[
                pl.BlockSpec((z.half, z.uc, LANES), lambda h, t: (h, jnp.maximum(t[LENT + way], 0) // z.nud, 0))
            ],
            out_specs=pl.BlockSpec((1, z.half, z.k), lambda h, t: (h, 0, 0)),
        ),
        out_shape=jax.ShapeDtypeStruct((2, z.half, z.k), jnp.bfloat16),
        compiler_params=pltpu.CompilerParams(vmem_limit_bytes=VMEM_LIMIT),
        name="lend_amps",
    )(table, amps)


def lend_integrals(z, table, integrals, way, part):
    ab = AB_BLOCK // 2
    steps = z.local_ab // 2 // ab

    def body(t, x_ref, y_ref, o_ref):
        unit = t[LENT + way]
        for second in range(z.nud):

            @pl.when((unit >= 0) & (lax.rem(unit, z.nud) == second))
            def _(second=second):
                def relay(i):
                    at = pl.ds(i * 32, 32)
                    o_ref[at] = squeeze_tile(second, x_ref[at], y_ref[at])

                each(ab // 32, relay)

    def imap(offset):
        return lambda j, t: (part * steps + j, jnp.maximum(t[LENT + way], 0) // z.nud * 2 + offset, 0)

    return pl.pallas_call(
        body,
        grid_spec=pltpu.PrefetchScalarGridSpec(
            num_scalar_prefetch=1,
            grid=(steps,),
            in_specs=[pl.BlockSpec((ab, z.rows, LANES), imap(0)), pl.BlockSpec((ab, z.rows, LANES), imap(1))],
            out_specs=pl.BlockSpec((ab, z.rows, LANES), lambda j, t: (j, 0, 0)),
        ),
        out_shape=jax.ShapeDtypeStruct((z.local_ab // 2, z.rows, LANES), jnp.bfloat16),
        compiler_params=pltpu.CompilerParams(vmem_limit_bytes=VMEM_LIMIT),
        name="lend_integrals",
    )(table, integrals, integrals)


def pack(z, table, amps, piece, borrowed=()):
    start = piece * PIECE
    given = swap_cores(pack_slots(z, table, amps, start, PIECE, False, borrowed))
    return pack_slots(z, table, amps, start, PIECE, True, borrowed, given)


def each(count, body):
    def step(i, carry):
        body(i)
        return carry

    lax.fori_loop(0, count, step, 0)


def ladder_piece(z, table, piece, gathered, integrals, total, borrowed=()):
    groups, count = gathered.shape[:2]
    swapped = swap_cores(gathered)
    ab = min(AB_BLOCK // 2 if borrowed else AB_BLOCK, z.local_ab)
    parts = z.local_ab // ab
    few, many, deep = 64, 256, min(z.k, 1024)
    per_unit = z.uc // z.rows
    split = z.rows % 16 == 0
    m = groups * z.half

    def by_lines(x):
        return x.reshape(-1, few, *x.shape[1:])

    def unit_of(t, s):
        return t[z.slot_mine + piece * PIECE + s]

    def tile(t, s):
        unit = unit_of(t, s)
        return jnp.where((unit >= 0) & (unit < z.units), unit, 0) // z.nud

    def body(t, g_ref, w_ref, prev_ref, *rest):
        lent_refs, rest = rest[: len(borrowed)], rest[len(borrowed) :]
        if split:
            x_ref, y_ref, out_ref, b_ref = rest
        else:
            x_ref, out_ref, b_ref = rest
        s = pl.program_id(1)
        unit = unit_of(t, s)

        @pl.when(s == 0)
        def _():
            out_ref[...] = prev_ref[...]

        for second in range(z.nud):

            @pl.when((unit >= 0) & (unit < z.units) & (lax.rem(unit, z.nud) == second))
            def _(second=second):
                def relay(i):
                    if split:
                        x, y = x_ref[i], y_ref[i]
                    else:
                        x, y = x_ref[i, :, : z.rows], x_ref[i, :, z.rows :]
                    b_ref[i] = squeeze_tile(second, x, y).reshape(few, z.k)

                each(ab // few, relay)

        for d in range(len(borrowed)):
            upper = pl.program_id(0) >= parts // 2

            @pl.when((unit == z.units + d // 2) & (upper == (d % 2 == 1)))
            def _(d=d):
                def relay(i):
                    b_ref[i] = lent_refs[d][i].reshape(few, z.k)

                each(ab // few, relay)

        @pl.when(unit >= 0)
        def _():
            def product(i):
                n, k = i // (z.k // deep), lax.rem(i, z.k // deep)
                at = pl.ds(pl.multiple_of(n * many, many), many)
                cols = pl.ds(pl.multiple_of(k * deep, deep), deep)
                b = b_ref[pl.ds(n * (many // few), many // few), :, cols].reshape(many, deep)
                for h, a_ref in enumerate((g_ref, w_ref)):
                    out_ref[h * m : (h + 1) * m, at] += lax.dot_general(
                        a_ref[:, 0, :, cols].reshape(m, deep),
                        b,
                        (((1,), (1,)), ((), ())),
                        preferred_element_type=jnp.float32,
                    )

            each((ab // many) * (z.k // deep), product)

    def imap(offset):
        def index(j, s, t):
            return (j, 0, tile(t, s) * per_unit + offset, 0)

        return index

    piece_spec = pl.BlockSpec((groups, 1, z.half, z.k), lambda j, s, t: (0, s, 0, 0))
    out_spec = pl.BlockSpec((groups * z.pairs, ab), lambda j, s, t: (0, j))
    if split:
        ints_specs = [pl.BlockSpec((ab // few, few, z.rows, LANES), imap(offset)) for offset in range(2)]
        ints = [by_lines(integrals)] * 2
    else:
        ints_specs = [pl.BlockSpec((ab // few, few, z.uc, LANES), lambda j, s, t: (j, 0, tile(t, s), 0))]
        ints = [by_lines(integrals)]
    low_spec = pl.BlockSpec((ab // few, few, z.rows, LANES), lambda j, s, t: (jnp.minimum(j, parts // 2 - 1), 0, 0, 0))
    high_spec = pl.BlockSpec((ab // few, few, z.rows, LANES), lambda j, s, t: (jnp.maximum(j - parts // 2, 0), 0, 0, 0))
    lent_specs = [low_spec, high_spec] * (len(borrowed) // 2)
    return pl.pallas_call(
        body,
        grid_spec=pltpu.PrefetchScalarGridSpec(
            num_scalar_prefetch=1,
            grid=(z.local_ab // ab, count),
            in_specs=[piece_spec, piece_spec, out_spec] + lent_specs + ints_specs,
            out_specs=out_spec,
            scratch_shapes=[pltpu.VMEM((ab // few, few, z.k), jnp.bfloat16)],
        ),
        out_shape=jax.ShapeDtypeStruct((groups * z.pairs, z.local_ab), jnp.float32),
        input_output_aliases={3: 0},
        compiler_params=pltpu.CompilerParams(vmem_limit_bytes=VMEM_LIMIT),
        cost_estimate=pl.CostEstimate(
            flops=2 * groups * z.pairs * z.local_ab * z.k * count,
            bytes_accessed=2 * z.local_ab * z.uc * LANES * count,
            transcendentals=0,
        ),
        name="ladder_piece",
    )(table, gathered, swapped, total, *[by_lines(x) for x in borrowed], *ints)


def swap_cores(x):
    return lax.ppermute(x, "col", [(i, i ^ 1) for i in range(lax.axis_size("col"))])


def over_row(x):
    return lax.ppermute(x, "row", [(0, 1), (1, 0)])


def over_chip(x):
    return lax.ppermute(x, "col", [(i, i ^ 2) for i in range(4)])


def pick(x, at, axis):
    return lax.dynamic_index_in_dim(x, at, axis, keepdims=False)


def reduce_plane(z, total):
    row, chip = lax.axis_index("row"), lax.axis_index("col") // 2

    def halve(x, at, axis, send):
        return pick(x, at, axis) + send(pick(x, 1 - at, axis))

    wide = z.local_ab // 2
    kept, given = total.reshape(2, 2, 2, z.half, z.local_ab)
    rest = kept + swap_cores(given)
    left, right = rest[..., :wide], rest[..., wide:]
    left = halve(left, row, 0, over_row)
    right = halve(right, chip, 1, over_chip)
    left = halve(left, chip, 0, over_chip)
    right = halve(right, row, 0, over_row)
    return jnp.concatenate([left, right], -1)


def per_device(amps, integrals, mask_amps, mask_ints):
    z = Sizes(amps, integrals)
    table = make_plan(z, mask_amps, mask_ints)
    groups = lax.axis_size("pair")

    def gather(own):
        return lax.all_gather(own, "pair")

    def add(piece, gathered, total, borrowed=()):
        return ladder_piece(z, table, piece, gathered, integrals, total, borrowed)

    def rare(total):
        return add(RARE, gather(pack(z, table, amps, RARE)), total)

    def finish(count, piece, own, second, total, borrowed):
        if count:
            last = gather(own[:count])
        if second is not None:
            total = add(SECOND, second, total, borrowed)
        if count:
            last, total = lax.optimization_barrier((last, total))
            total = add(piece, last, total)
        return total

    total = jnp.zeros((groups * z.pairs, z.local_ab), jnp.float32)
    head = pack(z, table, amps, HEAD)
    if z.long:
        first = gather(head)
        lent = over_chip(lend_amps(z, table, amps, 0)), over_row(lend_amps(z, table, amps, 1))
        ints = [[lend_integrals(z, table, integrals, way, part) for way in range(2)] for part in range(2)]
        lent, ints = lax.optimization_barrier((lent, ints))
        own = pack(z, table, amps, SECOND, lent)
        lower = over_chip(ints[0][0]), over_row(ints[0][1])
        third = pack(z, table, amps, THIRD)
        first, own, lower, third, rest = lax.optimization_barrier((first, own, lower, third, ints[1]))
        second = gather(own)
        upper = over_chip(rest[0]), over_row(rest[1])
        second, upper, total = lax.optimization_barrier((second, upper, add(HEAD, first, total)))
        borrowed = lower[0], upper[0], lower[1], upper[1]
        total = lax.cond(table[LONG] == 1, rare, lambda t: t, total)
        ends = [functools.partial(finish, n, THIRD) for n in range(PIECE + 1)]
        total = lax.switch(table[LAST], ends, third, second, total, borrowed)
    else:
        ends = [functools.partial(finish, n, HEAD) for n in range(1, PIECE + 1)]
        total = lax.switch(table[LAST] - 1, ends, head, None, total, ())

    if lax.axis_size("row") == 2 and lax.axis_size("col") == 4:
        ladder = lax.optimization_barrier(reduce_plane(z, total))
    else:
        halves = total.reshape(2, groups, z.half, z.local_ab)
        halves = jnp.where(table[CORE] == 0, halves, halves[::-1])
        total = jnp.swapaxes(halves, 0, 1).reshape(groups * z.pairs, z.local_ab)
        ladder = lax.psum_scatter(total, ("row", "col"), scatter_dimension=0, tiled=True)
    out_pairs = ladder.shape[0]
    local_a = WIN // groups
    grid = ladder.reshape(out_pairs, local_a, groups, local_a)
    received = lax.all_to_all(grid, "pair", split_axis=2, concat_axis=2, tiled=True)
    swapped = jnp.transpose(received, (0, 3, 2, 1)).reshape(out_pairs, local_a * WIN)
    return (0.5 * (ladder - swapped)).astype(jnp.bfloat16)


def solution(mesh):
    return jax.shard_map(
        per_device,
        mesh=mesh,
        in_specs=(P("pair", "row", "col"), P("pair", "row", "col"), P(), P()),
        out_specs=P(("row", "col"), "pair"),
        check_vma=False,
    )
```

profile of v0, /device:TPU:0, one launch (start us, length us, event | category | flops | bytes accessed | tf_op | source)
XLA Modules:
  0.0 494.1 jit_solution(10375649625453737476)
XLA Ops:
  15.4 3.8 collective-permute-done.11.refs_0_
  20.5 4.8 pack_kept.5
  34.6 7.2 %lend_integrals.4 = bf16[512,32,128]{2,1,0:T(8,128)(2,1)} custom-call(s32[48]{0:T(128)S(1)} %plan.1.t, bf16[1024,256,128]{2,1,0:T(8,128)(2,1)} %y_ref.7, bf16[1024,256,128]{2,1,0:T(8,128)(2,1)} %y_ref.7), custom_call_target="tpu_custom_call" | custom-call | tf_op jit(solution)/shard_map/lend_integrals/pallas_call | solution.py:265
  41.9 6.2 %lend_integrals.5 = bf16[512,32,128]{2,1,0:T(8,128)(2,1)} custom-call(s32[48]{0:T(128)S(1)} %plan.1.t, bf16[1024,256,128]{2,1,0:T(8,128)(2,1)} %y_ref.7, bf16[1024,256,128]{2,1,0:T(8,128)(2,1)} %y_ref.7), custom_call_target="tpu_custom_call" | custom-call | tf_op jit(solution)/shard_map/lend_integrals/pallas_call | solution.py:265
  48.0 6.4 %lend_integrals.6 = bf16[512,32,128]{2,1,0:T(8,128)(2,1)} custom-call(s32[48]{0:T(128)S(1)} %plan.1.t, bf16[1024,256,128]{2,1,0:T(8,128)(2,1)} %y_ref.7, bf16[1024,256,128]{2,1,0:T(8,128)(2,1)} %y_ref.7), custom_call_target="tpu_custom_call" | custom-call | tf_op jit(solution)/shard_map/lend_integrals/pallas_call | solution.py:265
  54.5 6.4 %lend_integrals.7 = bf16[512,32,128]{2,1,0:T(8,128)(2,1)} custom-call(s32[48]{0:T(128)S(1)} %plan.1.t, bf16[1024,256,128]{2,1,0:T(8,128)(2,1)} %y_ref.7, bf16[1024,256,128]{2,1,0:T(8,128)(2,1)} %y_ref.7), custom_call_target="tpu_custom_call" | custom-call | tf_op jit(solution)/shard_map/lend_integrals/pallas_call | solution.py:265
  63.9 5.7 %pack_given.6 = bf16[4,64,4096]{2,1,0:T(8,128)(2,1)} custom-call(s32[48]{0:T(128)S(1)} %plan.1.t, bf16[128,256,128]{2,1,0:T(8,128)(2,1)} %a_ref.15, bf16[2,64,4096]{2,1,0:T(8,128)(2,1)} %collective-permute-done.12.refs_0_, bf16[2,64,4096]{2,1,0:T(8,128)(2,1)} %collective-permute-done.13.refs_1_), custom_call_target="tpu_custom_call" | custom-call | bytes 8388608 | tf_op jit(solution)/shard_map/pack_given/pallas_call | solution.py:210
  70.1 4.2 pack_kept.7
  74.3 5.2 %pack_kept.6 = bf16[4,64,4096]{2,1,0:T(8,128)(2,1)} custom-call(s32[48]{0:T(128)S(1)} %plan.1.t, bf16[128,256,128]{2,1,0:T(8,128)(2,1)S(1)} %bitcast.73, bf16[2,64,4096]{2,1,0:T(8,128)(2,1)} %collective-permute-done.12.refs_0_, bf16[2,64,4096]{2,1,0:T(8,128)(2,1)} %collective-permute-done.13.refs_1_, bf16[4,64,4096]{2,1,0:T(8,128)(2,1)} %collective-permute-done.14.refs_2_), custom_call_target="tpu_custom_call" | custom-call | bytes 8388608 | tf_op jit(solution)/shard_map/pack_kept/pallas_call | solution.py:210
  79.5 75.0 %collective-permute-done.15 = bf16[512,32,128]{2,1,0:T(8,128)(2,1)} collective-permute-done((bf16[512,32,128]{2,1,0:T(8,128)(2,1)}, bf16[512,32,128]{2,1,0:T(8,128)(2,1)}, u32[]{:S(2)}, u32[]{:S(2)}) %collective-permute-start.15) | collective-permute-done | bytes 4194336 | tf_op jit(solution)/shard_map/ppermute | solution.py:413
  154.7 23.1 %all-gather.25.cloned.1.call-done = bf16[16,64,4096]{2,1,0:T(8,128)(2,1)} async-done(((bf16[4,64,4096]{2,1,0:T(8,128)(2,1)}), bf16[16,64,4096]{2,1,0:T(8,128)(2,1)}) %all-gather.25.cloned.1.call-update) | async-done | bytes 8388624 | tf_op jit(solution)/shard_map/all_gather | solution.py:443
  182.7 8.6 %collective-permute-done.20.w_ref = bf16[4,4,64,4096]{3,2,1,0:T(8,128)(2,1)S(1)} collective-permute-done((bf16[4,4,64,4096]{3,2,1,0:T(8,128)(2,1)}, bf16[4,4,64,4096]{3,2,1,0:T(8,128)(2,1)S(1)}, u32[]{:S(2)}, u32[]{:S(2)}) %collective-permute-start.20) | collective-permute-done | bytes 8388640 | tf_op jit(solution)/shard_map/ppermute | solution.py:405
  194.6 39.8 %ladder_piece.21 = f32[512,1024]{1,0:T(8,128)S(1)} custom-call(s32[48]{0:T(128)S(1)} %plan.1.t, bf16[4,4,64,4096]{3,2,1,0:T(8,128)(2,1)} %bitcast.80, bf16[4,4,64,4096]{3,2,1,0:T(8,128)(2,1)} %copy-done.4, f32[512,1024]{1,0:T(8,128)S(1)} %broadcast_in_dim.3.prev_ref, ...), custom_call_target="tpu_custom_call", output_to_operand_aliasing={{}: (3, {})} | custom-call | flops 17179869184 | bytes 67108864 | tf_op jit(solution)/shard_map/ladder_piece/pallas_call | solution.py:383
  234.4 36.8 %collective-permute-done.18 = bf16[512,32,128]{2,1,0:T(8,128)(2,1)} collective-permute-done((bf16[512,32,128]{2,1,0:T(8,128)(2,1)}, bf16[512,32,128]{2,1,0:T(8,128)(2,1)}, u32[]{:S(2)}, u32[]{:S(2)}) %collective-permute-start.18) | collective-permute-done | bytes 4194336 | tf_op jit(solution)/shard_map/ppermute | solution.py:413
  272.3 54.9 %all-gather.27.cloned.1.call-done = bf16[16,64,4096]{2,1,0:T(8,128)(2,1)} async-done(((bf16[4,64,4096]{2,1,0:T(8,128)(2,1)}), bf16[16,64,4096]{2,1,0:T(8,128)(2,1)}) %all-gather.27.cloned.1.call-update) | async-done | bytes 8388624 | tf_op jit(solution)/shard_map/all_gather | solution.py:443
  327.2 114.7 %conditional.3 = (f32[512,1024]{1,0:T(8,128)S(1)}) conditional(s32[]{:T(128)} %bitcast.33, (bf16[4,4,64,4096]{3,2,1,0:T(8,128)(2,1)}, bf16[512,32,128]{2,1,0:T(8,128)(2,1)}, bf16[512,32,128]{2,1,0:T(8,128)(2,1)}, bf16[512,32,128]{2,1,0:T(8,128)(2,1)}, bf16[512,32,128]{2,1,0:T(8,128)(2,1)}, ...), branch_computations={%region_2.0_spmd, %region_3.0_spmd, %region_4.0_spmd, %region_5.0_... | conditional | flops 34359738368 | bytes 299892896 | solution.py:478
  329.6 11.1 %collective-permute-done.5.w_ref = bf16[4,4,64,4096]{3,2,1,0:T(8,128)(2,1)} collective-permute-done((bf16[4,4,64,4096]{3,2,1,0:T(8,128)(2,1)}, bf16[4,4,64,4096]{3,2,1,0:T(8,128)(2,1)}, u32[]{:S(2)}, u32[]{:S(2)}) %collective-permute-start.5) | collective-permute-done | bytes 8388640 | tf_op jit(solution)/shard_map/cond/branch_2_fun/ppermute | solution.py:405
  340.7 59.7 %ladder_piece.15.prev_ref = f32[512,1024]{1,0:T(8,128)S(1)} custom-call(s32[48]{0:T(128)S(1)} %get-tuple-element.134.t, bf16[4,4,64,4096]{3,2,1,0:T(8,128)(2,1)} %get-tuple-element.136.g_ref, bf16[4,4,64,4096]{3,2,1,0:T(8,128)(2,1)} %collective-permute-done.5.w_ref, f32[512,1024]{1,0:T(8,128)S(1)} %get-tuple-element.137.prev_ref, ...), custom_call_target="tpu_custom_call", output_to_operand_aliasing={{}: (3, {})} | custom-call | flops 17179869184 | bytes 67108864 | tf_op jit(solution)/shard_map/cond/branch_2_fun/ladder_piece/pallas_call | solution.py:383
  400.4 8.5 %all-gather.19.cloned.1.call-done = bf16[8,64,4096]{2,1,0:T(8,128)(2,1)} async-done(((bf16[2,64,4096]{2,1,0:T(8,128)(2,1)}), bf16[8,64,4096]{2,1,0:T(8,128)(2,1)}) %all-gather.19.cloned.1.call-update) | async-done | bytes 4194320 | tf_op jit(solution)/shard_map/cond/branch_2_fun/all_gather | solution.py:443
  408.9 7.4 %collective-permute-done.6.w_ref = bf16[4,2,64,4096]{3,2,1,0:T(8,128)(2,1)S(1)} collective-permute-done((bf16[4,2,64,4096]{3,2,1,0:T(8,128)(2,1)}, bf16[4,2,64,4096]{3,2,1,0:T(8,128)(2,1)S(1)}, u32[]{:S(2)}, u32[]{:S(2)}) %collective-permute-start.6) | collective-permute-done | bytes 4194336 | tf_op jit(solution)/shard_map/cond/branch_2_fun/ppermute | solution.py:405
  418.3 23.4 %ladder_piece.16 = f32[512,1024]{1,0:T(8,128)S(1)} custom-call(s32[48]{0:T(128)S(1)} %get-tuple-element.134.t, bf16[4,2,64,4096]{3,2,1,0:T(8,128)(2,1)} %bitcast.89, bf16[4,2,64,4096]{3,2,1,0:T(8,128)(2,1)} %copy-done.10, f32[512,1024]{1,0:T(8,128)S(1)} %ladder_piece.15.prev_ref, ...), custom_call_target="tpu_custom_call", output_to_operand_aliasing={{}: (3, {})} | custom-call | flops 8589934592 | bytes 33554432 | tf_op jit(solution)/shard_map/cond/branch_2_fun/ladder_piece/pallas_call | solution.py:383
  452.8 11.2 %collective-permute-done.24 = f32[2,64,512]{1,2,0:T(8,128)S(1)} collective-permute-done((f32[2,64,512]{1,2,0:T(8,128)S(1)}, f32[2,64,512]{1,2,0:T(8,128)S(1)}, u32[]{:S(2)}, u32[]{:S(2)}) %collective-permute-start.24) | collective-permute-done | bytes 262176 | tf_op jit(solution)/shard_map/ppermute | solution.py:413
  467.4 4.9 %collective-permute-done.25 = f32[64,512]{0,1:T(8,128)S(1)} collective-permute-done((f32[64,512]{0,1:T(8,128)S(1)}, f32[64,512]{0,1:T(8,128)S(1)}, u32[]{:S(2)}, u32[]{:S(2)}) %collective-permute-start.25) | collective-permute-done | bytes 131104 | tf_op jit(solution)/shard_map/ppermute | solution.py:409
  474.8 9.5 %all_to_all.5 = f32[4,1,16384]{2,1,0:T(1,128)S(1)} all-to-all(f32[4,1,16384]{2,1,0:T(1,128)S(1)} %reshape.114), channel_id=1, replica_groups=mesh['row'=2,'col'=4,'pair'=4] {'pair'}, dimensions={0} | all-to-all | bytes 524288 | tf_op jit(solution)/shard_map/all_to_all | solution.py:493
  (87 shorter events, 55.6 us)
Async XLA Ops:
  6.5 171.2 %all-gather.25.cloned.1.call-start = ((), (), s32[]{:S(2)}) async-start(), calls=%async_computation.6 | async-start | bytes 10485760 | tf_op jit(solution)/shard_map/all_gather | solution.py:443
  10.7 9.8 %copy-start.1 = (bf16[128,256,128]{2,1,0:T(8,128)(2,1)S(1)}, bf16[128,256,128]{2,1,0:T(8,128)(2,1)}, u32[]{:S(2)}) copy-start(bf16[128,256,128]{2,1,0:T(8,128)(2,1)} %a_ref.15) | copy-start | bytes 25165828
  13.5 5.7 %collective-permute-start.11 = (bf16[4,64,4096]{2,1,0:T(8,128)(2,1)S(1)}, bf16[4,64,4096]{2,1,0:T(8,128)(2,1)S(1)}, u32[]{:S(2)}, u32[]{:S(2)}) collective-permute-start(bf16[4,64,4096]{2,1,0:T(8,128)(2,1)S(1)} %pack_given.5), channel_id=1, source_target_pairs={{0,4},{4,0},{8,12},{12,8},{1,5},{5,1},{9,13},{13,9},{2,6},{6,2},{1... | collective-permute-start | bytes 6291464 | tf_op jit(solution)/shard_map/ppermute | solution.py:405
  25.3 301.9 %all-gather.27.cloned.1.call-start = ((), (), s32[]{:S(2)}) async-start(), calls=%async_computation.7 | async-start | bytes 10485760 | tf_op jit(solution)/shard_map/all_gather | solution.py:443
  28.5 32.3 %collective-permute-start.12 = (bf16[2,64,4096]{2,1,0:T(8,128)(2,1)}, bf16[2,64,4096]{2,1,0:T(8,128)(2,1)}, u32[]{:S(2)}, u32[]{:S(2)}) collective-permute-start(bf16[2,64,4096]{2,1,0:T(8,128)(2,1)} %lend_amps.2), channel_id=1, source_target_pairs={{0,8},{4,12},{8,0},{12,4},{1,9},{5,13},{9,1},{13,5},{2,10},{6,14},... | collective-permute-start | bytes 3145736 | tf_op jit(solution)/shard_map/ppermute | solution.py:413
  32.5 28.3 %collective-permute-start.13 = (bf16[2,64,4096]{2,1,0:T(8,128)(2,1)}, bf16[2,64,4096]{2,1,0:T(8,128)(2,1)}, u32[]{:S(2)}, u32[]{:S(2)}) collective-permute-start(bf16[2,64,4096]{2,1,0:T(8,128)(2,1)} %lend_amps.3), channel_id=1, source_target_pairs={{0,16},{16,0},{1,17},{17,1},{2,18},{18,2},{3,19},{19,3},{4,20},{20... | collective-permute-start | bytes 3145736 | tf_op jit(solution)/shard_map/ppermute | solution.py:409
  48.0 14.5 %slice-start = ((s8[8388608]{0:T(1024)(128)(4,1)}), s8[4194304]{0:T(1024)(128)(4,1)S(1)}, s32[]{:S(2)}) async-start(s8[8388608]{0:T(1024)(128)(4,1)} %bitcast.70), calls=%async_computation.8 | async-start | bytes 8388608
  54.5 8.1 %slice-start.1 = ((s8[8388608]{0:T(1024)(128)(4,1)}), s8[4194304]{0:T(1024)(128)(4,1)S(1)}, s32[]{:S(2)}) async-start(s8[8388608]{0:T(1024)(128)(4,1)} %bitcast.70), calls=%async_computation.9 | async-start | bytes 8388608
  60.9 93.6 %collective-permute-start.15 = (bf16[512,32,128]{2,1,0:T(8,128)(2,1)}, bf16[512,32,128]{2,1,0:T(8,128)(2,1)}, u32[]{:S(2)}, u32[]{:S(2)}) collective-permute-start(bf16[512,32,128]{2,1,0:T(8,128)(2,1)} %lend_integrals.4), channel_id=1, source_target_pairs={{0,8},{4,12},{8,0},{12,4},{1,9},{5,13},{9,1},{13,5},{2,10},{6,14},... | collective-permute-start | bytes 12582920 | tf_op jit(solution)/shard_map/ppermute | solution.py:413
  62.3 92.4 %collective-permute-start.16 = (bf16[512,32,128]{2,1,0:T(8,128)(2,1)}, bf16[512,32,128]{2,1,0:T(8,128)(2,1)}, u32[]{:S(2)}, u32[]{:S(2)}) collective-permute-start(bf16[512,32,128]{2,1,0:T(8,128)(2,1)} %lend_integrals.5), channel_id=1, source_target_pairs={{0,16},{16,0},{1,17},{17,1},{2,18},{18,2},{3,19},{19,3},{4,20},{20... | collective-permute-start | bytes 12582920 | tf_op jit(solution)/shard_map/ppermute | solution.py:409
  63.8 6.3 %collective-permute-start.17 = (bf16[4,64,4096]{2,1,0:T(8,128)(2,1)S(1)}, bf16[4,64,4096]{2,1,0:T(8,128)(2,1)S(1)}, u32[]{:S(2)}, u32[]{:S(2)}) collective-permute-start(bf16[4,64,4096]{2,1,0:T(8,128)(2,1)S(1)} %pack_given.7), channel_id=1, source_target_pairs={{0,4},{4,0},{8,12},{12,8},{1,5},{5,1},{9,13},{13,9},{2,6},{6,2},{1... | collective-permute-start | bytes 6291464 | tf_op jit(solution)/shard_map/ppermute | solution.py:405
  63.9 10.4 %slice-start.2 = ((s8[8388608]{0:T(1024)(128)(4,1)}), s8[4194304]{0:T(1024)(128)(4,1)S(1)}, s32[]{:S(2)}) async-start(s8[8388608]{0:T(1024)(128)(4,1)} %bitcast.72), calls=%async_computation.10 | async-start | bytes 8388608
  69.6 4.7 collective-permute-start.14
  177.8 13.4 %collective-permute-start.20 = (bf16[4,4,64,4096]{3,2,1,0:T(8,128)(2,1)}, bf16[4,4,64,4096]{3,2,1,0:T(8,128)(2,1)S(1)}, u32[]{:S(2)}, u32[]{:S(2)}) collective-permute-start(bf16[4,4,64,4096]{3,2,1,0:T(8,128)(2,1)} %bitcast.79), channel_id=1, source_target_pairs={{0,4},{4,0},{8,12},{12,8},{1,5},{5,1},{9,13},{13,9},{2,6},{6,2},{1... | collective-permute-start | bytes 25165832 | tf_op jit(solution)/shard_map/ppermute | solution.py:405
  177.9 93.3 %collective-permute-start.18 = (bf16[512,32,128]{2,1,0:T(8,128)(2,1)}, bf16[512,32,128]{2,1,0:T(8,128)(2,1)}, u32[]{:S(2)}, u32[]{:S(2)}) collective-permute-start(bf16[512,32,128]{2,1,0:T(8,128)(2,1)} %lend_integrals.6), channel_id=1, source_target_pairs={{0,8},{4,12},{8,0},{12,4},{1,9},{5,13},{9,1},{13,5},{2,10},{6,14},... | collective-permute-start | bytes 12582920 | tf_op jit(solution)/shard_map/ppermute | solution.py:413
  179.4 93.0 %collective-permute-start.19 = (bf16[512,32,128]{2,1,0:T(8,128)(2,1)}, bf16[512,32,128]{2,1,0:T(8,128)(2,1)}, u32[]{:S(2)}, u32[]{:S(2)}) collective-permute-start(bf16[512,32,128]{2,1,0:T(8,128)(2,1)} %lend_integrals.7), channel_id=1, source_target_pairs={{0,16},{16,0},{1,17},{17,1},{2,18},{18,2},{3,19},{19,3},{4,20},{20... | collective-permute-start | bytes 12582920 | tf_op jit(solution)/shard_map/ppermute | solution.py:409
  327.2 81.7 %all-gather.19.cloned.1.call-start = ((), (), s32[]{:S(2)}) async-start(), calls=%async_computation.3 | async-start | bytes 5242880 | tf_op jit(solution)/shard_map/cond/branch_2_fun/all_gather | solution.py:443
  327.2 13.5 %collective-permute-start.5 = (bf16[4,4,64,4096]{3,2,1,0:T(8,128)(2,1)}, bf16[4,4,64,4096]{3,2,1,0:T(8,128)(2,1)}, u32[]{:S(2)}, u32[]{:S(2)}) collective-permute-start(bf16[4,4,64,4096]{3,2,1,0:T(8,128)(2,1)} %get-tuple-element.136.g_ref), channel_id=1, source_target_pairs={{0,4},{4,0},{8,12},{12,8},{1,5},{5,1},{9,13},{13,9},{2,6},{6,2},{1... | collective-permute-start | bytes 25165832 | tf_op jit(solution)/shard_map/cond/branch_2_fun/ppermute | solution.py:405
  408.9 7.4 %collective-permute-start.6 = (bf16[4,2,64,4096]{3,2,1,0:T(8,128)(2,1)}, bf16[4,2,64,4096]{3,2,1,0:T(8,128)(2,1)S(1)}, u32[]{:S(2)}, u32[]{:S(2)}) collective-permute-start(bf16[4,2,64,4096]{3,2,1,0:T(8,128)(2,1)} %bitcast.88), channel_id=1, source_target_pairs={{0,4},{4,0},{8,12},{12,8},{1,5},{5,1},{9,13},{13,9},{2,6},{6,2},{1... | collective-permute-start | bytes 12582920 | tf_op jit(solution)/shard_map/cond/branch_2_fun/ppermute | solution.py:405
  443.1 6.1 %collective-permute-start.21 = (f32[2,2,64,1024]{3,2,1,0:T(8,128)}, f32[2,2,64,1024]{3,2,1,0:T(8,128)S(1)}, u32[]{:S(2)}, u32[]{:S(2)}) collective-permute-start(f32[2,2,64,1024]{3,2,1,0:T(8,128)} %bitcast.39), channel_id=1, source_target_pairs={{0,4},{4,0},{8,12},{12,8},{1,5},{5,1},{9,13},{13,9},{2,6},{6,2},{1... | collective-permute-start | bytes 3145736 | tf_op jit(solution)/shard_map/ppermute | solution.py:405
  449.7 14.3 %collective-permute-start.24 = (f32[2,64,512]{1,2,0:T(8,128)S(1)}, f32[2,64,512]{1,2,0:T(8,128)S(1)}, u32[]{:S(2)}, u32[]{:S(2)}) collective-permute-start(f32[2,64,512]{1,2,0:T(8,128)S(1)} %bitcast.92), channel_id=1, source_target_pairs={{0,8},{4,12},{8,0},{12,4},{1,9},{5,13},{9,1},{13,5},{2,10},{6,14},... | collective-permute-start | bytes 786440 | tf_op jit(solution)/shard_map/ppermute | solution.py:413
  452.6 14.5 %collective-permute-start.22 = (f32[2,64,512]{1,2,0:T(8,128)}, f32[2,64,512]{1,2,0:T(8,128)S(1)}, u32[]{:S(2)}, u32[]{:S(2)}) collective-permute-start(f32[2,64,512]{1,2,0:T(8,128)} %bitcast.41), channel_id=1, source_target_pairs={{0,16},{16,0},{1,17},{17,1},{2,18},{18,2},{3,19},{19,3},{4,20},{20... | collective-permute-start | bytes 786440 | tf_op jit(solution)/shard_map/ppermute | solution.py:409
  464.1 8.3 %collective-permute-start.25 = (f32[64,512]{0,1:T(8,128)S(1)}, f32[64,512]{0,1:T(8,128)S(1)}, u32[]{:S(2)}, u32[]{:S(2)}) collective-permute-start(f32[64,512]{0,1:T(8,128)S(1)} %dynamic-slice_bitcast_fusion), channel_id=1, source_target_pairs={{0,16},{16,0},{1,17},{17,1},{2,18},{18,2},{3,19},{19,3},{4,20},{20... | collective-permute-start | bytes 393224 | tf_op jit(solution)/shard_map/ppermute | solution.py:409
  467.2 7.2 %collective-permute-start.23 = (f32[64,512]{0,1:T(8,128)S(1)}, f32[64,512]{0,1:T(8,128)S(1)}, u32[]{:S(2)}, u32[]{:S(2)}) collective-permute-start(f32[64,512]{0,1:T(8,128)S(1)} %dynamic-slice_bitcast_fusion.1), channel_id=1, source_target_pairs={{0,8},{4,12},{8,0},{12,4},{1,9},{5,13},{9,1},{13,5},{2,10},{6,14},... | collective-permute-start | bytes 393224 | tf_op jit(solution)/shard_map/ppermute | solution.py:413
  (5 other events, 16.8 us)
Sparse Core Ops, SparseCore 0:
  25.5 152.2 all-gather.24
  179.3 147.8 all-gather.26
  329.8 79.0 all-gather.18
where the time goes:
time: 494 us
  waiting for transfers between devices  254 us (51%)
  Pallas kernels  181 us (37%)
  starting transfers between devices  17.5 us (4%)
  local copies, waits for them, and re-layouts  14.8 us (3%)
  between operations  14.5 us (3%)
  blocking collectives  9.51 us (2%)
    ppermute x5, waiting for transfers between devices, over_chip(): return lax.ppermute(x, 'col', [(i, i ^ 2) for i in range(4)])  125 us
    pallas_call x3, Pallas kernels, ladder_piece(): pl.pallas_call(body, grid_spec=pltpu.PrefetchScalarGridSpec(num_scalar_pr...  123 us
    all_gather x3, waiting for transfers between devices, gather(): return lax.all_gather(own, 'pair')  86.4 us
    ppermute x7, waiting for transfers between devices, swap_cores(): lax.ppermute(x, 'col', [(i, i ^ 1) for i in range(lax.axis_size('col'))])  33.3 us
    pallas_call x4, Pallas kernels, lend_integrals(): pl.pallas_call(body, grid_spec=pltpu.PrefetchScalarGridSpec(num_scalar_pr...  26.2 us
    pallas_call x6, Pallas kernels, pack_slots(): pl.pallas_call(body, grid_spec=pltpu.PrefetchScalarGridSpec(num_scalar_pr...  24 us
  transfers between devices with their start and end apart: 20, of which 16 were waited for; matrix products, arithmetic and copies ran while one was open for 1% of the time, Pallas kernels for 30%

commit v1 on v0

--- a/solution.py
+++ b/solution.py
@@ -34,7 +34,9 @@
         self.places = (4 if self.long else 1) * PIECE
         self.slot_mine = UNITS + self.units
         self.slot_other = self.slot_mine + self.places
-        self.table = self.slot_other + self.places
+        self.fetch = self.slot_other + self.places
+        self.fetch_tile = self.fetch + self.places
+        self.table = self.fetch_tile + self.places
 
 
 def lending(counts, here, there):
@@ -139,6 +141,21 @@
             theirs |= borrowed & (core != j % 2)
         table_ref[z.slot_mine + at] = mine
         table_ref[z.slot_other + at] = jnp.where(theirs, 1, 0)
+    for start in range(0, z.places, PIECE):
+        units = [table_ref[z.slot_mine + start + j] for j in range(PIECE)]
+        for place, limit in ((z.fetch, z.units + 2), (z.fetch_tile, z.units)):
+            used = [(u >= 0) & (u < limit) for u in units]
+            last = zero
+            for j in reversed(range(PIECE)):
+                last = jnp.where(used[j], j, last)
+            for j in range(PIECE):
+                last = jnp.where(used[j], j, last)
+                if place == z.fetch:
+                    table_ref[place + start + j] = last
+                else:
+                    unit = table_ref[z.slot_mine + start + last]
+                    unit = jnp.where((unit >= 0) & (unit < limit), unit, 0)
+                    table_ref[place + start + j] = unit // z.nud
 
 
 def make_plan(z, mask_amps, mask_ints):
@@ -307,8 +324,7 @@
         return t[z.slot_mine + piece * PIECE + s]
 
     def tile(t, s):
-        unit = unit_of(t, s)
-        return jnp.where((unit >= 0) & (unit < z.units), unit, 0) // z.nud
+        return t[z.fetch_tile + piece * PIECE + s]
 
     def body(t, g_ref, w_ref, prev_ref, *rest):
         lent_refs, rest = rest[: len(borrowed)], rest[len(borrowed) :]
@@ -369,7 +385,7 @@
 
         return index
 
-    piece_spec = pl.BlockSpec((groups, 1, z.half, z.k), lambda j, s, t: (0, s, 0, 0))
+    piece_spec = pl.BlockSpec((groups, 1, z.half, z.k), lambda j, s, t: (0, t[z.fetch + piece * PIECE + s], 0, 0))
     out_spec = pl.BlockSpec((groups * z.pairs, ab), lambda j, s, t: (0, j))
     if split:
         ints_specs = [pl.BlockSpec((ab // few, few, z.rows, LANES), imap(offset)) for offset in range(2)]

time: 494 us -> 475 us (0.962)
  waiting for transfers between devices: 254 us -> 231 us
  starting transfers between devices: 17.5 us -> 37.7 us
  Pallas kernels: 181 us -> 163 us
    pallas_call x3, Pallas kernels: 123 us -> 103 us  [ladder_piece(): pl.pallas_call(body, grid_spec=pltpu.PrefetchScalarGridSpec(num_scalar_pr...]
    ppermute x5, starting transfers between devices: 6.96 us -> 18.3 us  [over_chip(): return lax.ppermute(x, 'col', [(i, i ^ 2) for i in range(4)])]
    ppermute x5, waiting for transfers between devices: 125 us -> 114 us  [over_chip(): return lax.ppermute(x, 'col', [(i, i ^ 2) for i in range(4)])]
    all_gather x3, waiting for transfers between devices: 86.4 us -> 77 us  [gather(): return lax.all_gather(own, 'pair')]
where the time goes in v1:
time: 475 us
  waiting for transfers between devices  231 us (49%)
  Pallas kernels  163 us (34%)
  starting transfers between devices  37.7 us (8%)
  local copies, waits for them, and re-layouts  15.3 us (3%)
  between operations  14.5 us (3%)
  blocking collectives  10.2 us (2%)
    ppermute x5, waiting for transfers between devices, over_chip(): return lax.ppermute(x, 'col', [(i, i ^ 2) for i in range(4)])  114 us
    pallas_call x3, Pallas kernels, ladder_piece(): pl.pallas_call(body, grid_spec=pltpu.PrefetchScalarGridSpec(num_scalar_pr...  103 us
    all_gather x3, waiting for transfers between devices, gather(): return lax.all_gather(own, 'pair')  77 us
    ppermute x7, waiting for transfers between devices, swap_cores(): lax.ppermute(x, 'col', [(i, i ^ 1) for i in range(lax.axis_size('col'))])  31.6 us
    pallas_call x4, Pallas kernels, lend_integrals(): pl.pallas_call(body, grid_spec=pltpu.PrefetchScalarGridSpec(num_scalar_pr...  26.2 us
    pallas_call x6, Pallas kernels, pack_slots(): pl.pallas_call(body, grid_spec=pltpu.PrefetchScalarGridSpec(num_scalar_pr...  25.4 us
    ppermute x5, starting transfers between devices, over_chip(): return lax.ppermute(x, 'col', [(i, i ^ 2) for i in range(4)])  18.3 us
    ppermute x7, starting transfers between devices, swap_cores(): lax.ppermute(x, 'col', [(i, i ^ 1) for i in range(lax.axis_size('col'))])  10.4 us
  transfers between devices with their start and end apart: 20, of which 16 were waited for; matrix products, arithmetic and copies ran while one was open for 1% of the time, Pallas kernels for 30%

profile of v1, /device:TPU:0, one launch (start us, length us, event | category | flops | bytes accessed | tf_op | source)
XLA Modules:
  0.0 475.4 jit_solution(8722169212233741650)
XLA Ops:
  10.9 4.3 pack_given.5
  20.7 4.8 %pack_kept.5 = bf16[4,64,4096]{2,1,0:T(8,128)(2,1)} custom-call(s32[80]{0:T(128)S(1)} %plan.1.t, bf16[128,256,128]{2,1,0:T(8,128)(2,1)S(1)} %copy-done.1, bf16[4,64,4096]{2,1,0:T(8,128)(2,1)} %copy-done.12), custom_call_target="tpu_custom_call" | custom-call | bytes 8388608 | tf_op jit(solution)/shard_map/pack_kept/pallas_call | solution.py:227
  34.8 7.2 %lend_integrals.4 = bf16[512,32,128]{2,1,0:T(8,128)(2,1)} custom-call(s32[80]{0:T(128)S(1)} %plan.1.t, bf16[1024,256,128]{2,1,0:T(8,128)(2,1)} %y_ref.7, bf16[1024,256,128]{2,1,0:T(8,128)(2,1)} %y_ref.7), custom_call_target="tpu_custom_call" | custom-call | tf_op jit(solution)/shard_map/lend_integrals/pallas_call | solution.py:282
  42.1 6.2 %lend_integrals.5 = bf16[512,32,128]{2,1,0:T(8,128)(2,1)} custom-call(s32[80]{0:T(128)S(1)} %plan.1.t, bf16[1024,256,128]{2,1,0:T(8,128)(2,1)} %y_ref.7, bf16[1024,256,128]{2,1,0:T(8,128)(2,1)} %y_ref.7), custom_call_target="tpu_custom_call" | custom-call | tf_op jit(solution)/shard_map/lend_integrals/pallas_call | solution.py:282
  48.2 6.4 %lend_integrals.6 = bf16[512,32,128]{2,1,0:T(8,128)(2,1)} custom-call(s32[80]{0:T(128)S(1)} %plan.1.t, bf16[1024,256,128]{2,1,0:T(8,128)(2,1)} %y_ref.7, bf16[1024,256,128]{2,1,0:T(8,128)(2,1)} %y_ref.7), custom_call_target="tpu_custom_call" | custom-call | tf_op jit(solution)/shard_map/lend_integrals/pallas_call | solution.py:282
  54.7 6.4 %lend_integrals.7 = bf16[512,32,128]{2,1,0:T(8,128)(2,1)} custom-call(s32[80]{0:T(128)S(1)} %plan.1.t, bf16[1024,256,128]{2,1,0:T(8,128)(2,1)} %y_ref.7, bf16[1024,256,128]{2,1,0:T(8,128)(2,1)} %y_ref.7), custom_call_target="tpu_custom_call" | custom-call | tf_op jit(solution)/shard_map/lend_integrals/pallas_call | solution.py:282
  64.3 6.0 %pack_given.6 = bf16[4,64,4096]{2,1,0:T(8,128)(2,1)} custom-call(s32[80]{0:T(128)S(1)} %plan.1.t, bf16[128,256,128]{2,1,0:T(8,128)(2,1)} %a_ref.15, bf16[2,64,4096]{2,1,0:T(8,128)(2,1)} %collective-permute-done.12.refs_0_, bf16[2,64,4096]{2,1,0:T(8,128)(2,1)} %collective-permute-done.13.refs_1_), custom_call_target="tpu_custom_call" | custom-call | bytes 8388608 | tf_op jit(solution)/shard_map/pack_given/pallas_call | solution.py:227
  74.9 5.5 %pack_kept.6 = bf16[4,64,4096]{2,1,0:T(8,128)(2,1)} custom-call(s32[80]{0:T(128)S(1)} %plan.1.t, bf16[128,256,128]{2,1,0:T(8,128)(2,1)S(1)} %bitcast.73, bf16[2,64,4096]{2,1,0:T(8,128)(2,1)} %collective-permute-done.12.refs_0_, bf16[2,64,4096]{2,1,0:T(8,128)(2,1)} %collective-permute-done.13.refs_1_, bf16[4,64,4096]{2,1,0:T(8,128)(2,1)} %collective-permute-done.14.refs_2_), custom_call_target="tpu_custom_call" | custom-call | bytes 8388608 | tf_op jit(solution)/shard_map/pack_kept/pallas_call | solution.py:227
  80.3 74.0 %collective-permute-done.15 = bf16[512,32,128]{2,1,0:T(8,128)(2,1)} collective-permute-done((bf16[512,32,128]{2,1,0:T(8,128)(2,1)}, bf16[512,32,128]{2,1,0:T(8,128)(2,1)}, u32[]{:S(2)}, u32[]{:S(2)}) %collective-permute-start.15) | collective-permute-done | bytes 4194336 | tf_op jit(solution)/shard_map/ppermute | solution.py:429
  155.8 22.1 %all-gather.25.cloned.1.call-done = bf16[16,64,4096]{2,1,0:T(8,128)(2,1)} async-done(((bf16[4,64,4096]{2,1,0:T(8,128)(2,1)}), bf16[16,64,4096]{2,1,0:T(8,128)(2,1)}) %all-gather.25.cloned.1.call-update) | async-done | bytes 8388624 | tf_op jit(solution)/shard_map/all_gather | solution.py:459
  182.8 8.6 %collective-permute-done.20.w_ref = bf16[4,4,64,4096]{3,2,1,0:T(8,128)(2,1)S(1)} collective-permute-done((bf16[4,4,64,4096]{3,2,1,0:T(8,128)(2,1)}, bf16[4,4,64,4096]{3,2,1,0:T(8,128)(2,1)S(1)}, u32[]{:S(2)}, u32[]{:S(2)}) %collective-permute-start.20) | collective-permute-done | bytes 8388640 | tf_op jit(solution)/shard_map/ppermute | solution.py:421
  194.7 47.3 %ladder_piece.21 = f32[512,1024]{1,0:T(8,128)S(1)} custom-call(s32[80]{0:T(128)S(1)} %plan.1.t, bf16[4,4,64,4096]{3,2,1,0:T(8,128)(2,1)} %bitcast.80, bf16[4,4,64,4096]{3,2,1,0:T(8,128)(2,1)} %copy-done.4, f32[512,1024]{1,0:T(8,128)S(1)} %broadcast_in_dim.3.prev_ref, ...), custom_call_target="tpu_custom_call", output_to_operand_aliasing={{}: (3, {})} | custom-call | flops 17179869184 | bytes 67108864 | tf_op jit(solution)/shard_map/ladder_piece/pallas_call | solution.py:399
  242.1 29.3 %collective-permute-done.18 = bf16[512,32,128]{2,1,0:T(8,128)(2,1)} collective-permute-done((bf16[512,32,128]{2,1,0:T(8,128)(2,1)}, bf16[512,32,128]{2,1,0:T(8,128)(2,1)}, u32[]{:S(2)}, u32[]{:S(2)}) %collective-permute-start.18) | collective-permute-done | bytes 4194336 | tf_op jit(solution)/shard_map/ppermute | solution.py:429
  272.5 54.9 %all-gather.27.cloned.1.call-done = bf16[16,64,4096]{2,1,0:T(8,128)(2,1)} async-done(((bf16[4,64,4096]{2,1,0:T(8,128)(2,1)}), bf16[16,64,4096]{2,1,0:T(8,128)(2,1)}) %all-gather.27.cloned.1.call-update) | async-done | bytes 8388624 | tf_op jit(solution)/shard_map/all_gather | solution.py:459
  327.4 77.2 %conditional.3 = (f32[512,1024]{1,0:T(8,128)S(1)}) conditional(s32[]{:T(128)} %bitcast.33, (bf16[4,4,64,4096]{3,2,1,0:T(8,128)(2,1)}, bf16[512,32,128]{2,1,0:T(8,128)(2,1)}, bf16[512,32,128]{2,1,0:T(8,128)(2,1)}, bf16[512,32,128]{2,1,0:T(8,128)(2,1)}, bf16[512,32,128]{2,1,0:T(8,128)(2,1)}, ...), branch_computations={%region_2.0_spmd, %region_3.0_spmd, %region_4.0_spmd, %region_5.0_... | conditional | flops 34359738368 | bytes 299892896 | solution.py:494
  329.4 11.5 %collective-permute-done.3.w_ref = bf16[4,4,64,4096]{3,2,1,0:T(8,128)(2,1)} collective-permute-done((bf16[4,4,64,4096]{3,2,1,0:T(8,128)(2,1)}, bf16[4,4,64,4096]{3,2,1,0:T(8,128)(2,1)}, u32[]{:S(2)}, u32[]{:S(2)}) %collective-permute-start.3) | collective-permute-done | bytes 8388640 | tf_op jit(solution)/shard_map/cond/branch_1_fun/ppermute | solution.py:421
  340.9 48.6 %ladder_piece.13.prev_ref = f32[512,1024]{1,0:T(8,128)S(1)} custom-call(s32[80]{0:T(128)S(1)} %get-tuple-element.123.t, bf16[4,4,64,4096]{3,2,1,0:T(8,128)(2,1)} %get-tuple-element.125.g_ref, bf16[4,4,64,4096]{3,2,1,0:T(8,128)(2,1)} %collective-permute-done.3.w_ref, f32[512,1024]{1,0:T(8,128)S(1)} %get-tuple-element.126.prev_ref, ...), custom_call_target="tpu_custom_call", output_to_operand_aliasing={{}: (3, {})} | custom-call | flops 17179869184 | bytes 67108864 | tf_op jit(solution)/shard_map/cond/branch_1_fun/ladder_piece/pallas_call | solution.py:399
  389.6 4.4 collective-permute-done.4.w_ref
  396.9 7.4 %ladder_piece.14 = f32[512,1024]{1,0:T(8,128)S(1)} custom-call(s32[80]{0:T(128)S(1)} %get-tuple-element.123.t, bf16[4,1,64,4096]{3,2,1,0:T(8,128)(2,1)S(1)} %bitcast.69, bf16[4,1,64,4096]{3,2,1,0:T(8,128)(2,1)} %copy-done.11, f32[512,1024]{1,0:T(8,128)S(1)} %ladder_piece.13.prev_ref, ...), custom_call_target="tpu_custom_call", output_to_operand_aliasing={{}: (3, {})} | custom-call | flops 4294967296 | bytes 16777216 | tf_op jit(solution)/shard_map/cond/branch_1_fun/ladder_piece/pallas_call | solution.py:399
  405.8 9.5 %collective-permute-start.21 = (f32[2,2,64,1024]{3,2,1,0:T(8,128)}, f32[2,2,64,1024]{3,2,1,0:T(8,128)S(1)}, u32[]{:S(2)}, u32[]{:S(2)}) collective-permute-start(f32[2,2,64,1024]{3,2,1,0:T(8,128)} %bitcast.39), channel_id=1, source_target_pairs={{0,4},{4,0},{8,12},{12,8},{1,5},{5,1},{9,13},{13,9},{2,6},{6,2},{1... | collective-permute-start | bytes 3145736 | tf_op jit(solution)/shard_map/ppermute | solution.py:421
  418.3 12.4 %collective-permute-start.24 = (f32[2,64,512]{1,2,0:T(8,128)S(1)}, f32[2,64,512]{1,2,0:T(8,128)S(1)}, u32[]{:S(2)}, u32[]{:S(2)}) collective-permute-start(f32[2,64,512]{1,2,0:T(8,128)S(1)} %bitcast.92), channel_id=1, source_target_pairs={{0,8},{4,12},{8,0},{12,4},{1,9},{5,13},{9,1},{13,5},{2,10},{6,14},... | collective-permute-start | bytes 786440 | tf_op jit(solution)/shard_map/ppermute | solution.py:429
  434.9 8.3 %collective-permute-done.24 = f32[2,64,512]{1,2,0:T(8,128)S(1)} collective-permute-done((f32[2,64,512]{1,2,0:T(8,128)S(1)}, f32[2,64,512]{1,2,0:T(8,128)S(1)}, u32[]{:S(2)}, u32[]{:S(2)}) %collective-permute-start.24) | collective-permute-done | bytes 262176 | tf_op jit(solution)/shard_map/ppermute | solution.py:429
  447.9 4.8 %collective-permute-done.25 = f32[64,512]{0,1:T(8,128)S(1)} collective-permute-done((f32[64,512]{0,1:T(8,128)S(1)}, f32[64,512]{0,1:T(8,128)S(1)}, u32[]{:S(2)}, u32[]{:S(2)}) %collective-permute-start.25) | collective-permute-done | bytes 131104 | tf_op jit(solution)/shard_map/ppermute | solution.py:425
  455.4 10.2 %all_to_all.5 = f32[4,1,16384]{2,1,0:T(1,128)S(1)} all-to-all(f32[4,1,16384]{2,1,0:T(1,128)S(1)} %reshape.114), channel_id=1, replica_groups=mesh['row'=2,'col'=4,'pair'=4] {'pair'}, dimensions={0} | all-to-all | bytes 524288 | tf_op jit(solution)/shard_map/all_to_all | solution.py:509
  (89 shorter events, 60.5 us)
Async XLA Ops:
  6.5 171.4 %all-gather.25.cloned.1.call-start = ((), (), s32[]{:S(2)}) async-start(), calls=%async_computation.6 | async-start | bytes 10485760 | tf_op jit(solution)/shard_map/all_gather | solution.py:459
  10.9 9.8 %copy-start.1 = (bf16[128,256,128]{2,1,0:T(8,128)(2,1)S(1)}, bf16[128,256,128]{2,1,0:T(8,128)(2,1)}, u32[]{:S(2)}) copy-start(bf16[128,256,128]{2,1,0:T(8,128)(2,1)} %a_ref.15) | copy-start | bytes 25165828
  15.2 4.2 collective-permute-start.11
  25.5 301.9 %all-gather.27.cloned.1.call-start = ((), (), s32[]{:S(2)}) async-start(), calls=%async_computation.7 | async-start | bytes 10485760 | tf_op jit(solution)/shard_map/all_gather | solution.py:459
  28.7 32.3 %collective-permute-start.12 = (bf16[2,64,4096]{2,1,0:T(8,128)(2,1)}, bf16[2,64,4096]{2,1,0:T(8,128)(2,1)}, u32[]{:S(2)}, u32[]{:S(2)}) collective-permute-start(bf16[2,64,4096]{2,1,0:T(8,128)(2,1)} %lend_amps.2), channel_id=1, source_target_pairs={{0,8},{4,12},{8,0},{12,4},{1,9},{5,13},{9,1},{13,5},{2,10},{6,14},... | collective-permute-start | bytes 3145736 | tf_op jit(solution)/shard_map/ppermute | solution.py:429
  33.0 28.0 %collective-permute-start.13 = (bf16[2,64,4096]{2,1,0:T(8,128)(2,1)}, bf16[2,64,4096]{2,1,0:T(8,128)(2,1)}, u32[]{:S(2)}, u32[]{:S(2)}) collective-permute-start(bf16[2,64,4096]{2,1,0:T(8,128)(2,1)} %lend_amps.3), channel_id=1, source_target_pairs={{0,16},{16,0},{1,17},{17,1},{2,18},{18,2},{3,19},{19,3},{4,20},{20... | collective-permute-start | bytes 3145736 | tf_op jit(solution)/shard_map/ppermute | solution.py:425
  48.2 14.7 %slice-start = ((s8[8388608]{0:T(1024)(128)(4,1)}), s8[4194304]{0:T(1024)(128)(4,1)S(1)}, s32[]{:S(2)}) async-start(s8[8388608]{0:T(1024)(128)(4,1)} %bitcast.70), calls=%async_computation.8 | async-start | bytes 8388608
  54.7 8.3 %slice-start.1 = ((s8[8388608]{0:T(1024)(128)(4,1)}), s8[4194304]{0:T(1024)(128)(4,1)S(1)}, s32[]{:S(2)}) async-start(s8[8388608]{0:T(1024)(128)(4,1)} %bitcast.70), calls=%async_computation.9 | async-start | bytes 8388608
  61.1 93.3 %collective-permute-start.15 = (bf16[512,32,128]{2,1,0:T(8,128)(2,1)}, bf16[512,32,128]{2,1,0:T(8,128)(2,1)}, u32[]{:S(2)}, u32[]{:S(2)}) collective-permute-start(bf16[512,32,128]{2,1,0:T(8,128)(2,1)} %lend_integrals.4), channel_id=1, source_target_pairs={{0,8},{4,12},{8,0},{12,4},{1,9},{5,13},{9,1},{13,5},{2,10},{6,14},... | collective-permute-start | bytes 12582920 | tf_op jit(solution)/shard_map/ppermute | solution.py:429
  62.4 93.4 %collective-permute-start.16 = (bf16[512,32,128]{2,1,0:T(8,128)(2,1)}, bf16[512,32,128]{2,1,0:T(8,128)(2,1)}, u32[]{:S(2)}, u32[]{:S(2)}) collective-permute-start(bf16[512,32,128]{2,1,0:T(8,128)(2,1)} %lend_integrals.5), channel_id=1, source_target_pairs={{0,16},{16,0},{1,17},{17,1},{2,18},{18,2},{3,19},{19,3},{4,20},{20... | collective-permute-start | bytes 12582920 | tf_op jit(solution)/shard_map/ppermute | solution.py:425
  63.8 6.6 %collective-permute-start.17 = (bf16[4,64,4096]{2,1,0:T(8,128)(2,1)S(1)}, bf16[4,64,4096]{2,1,0:T(8,128)(2,1)S(1)}, u32[]{:S(2)}, u32[]{:S(2)}) collective-permute-start(bf16[4,64,4096]{2,1,0:T(8,128)(2,1)S(1)} %pack_given.7), channel_id=1, source_target_pairs={{0,4},{4,0},{8,12},{12,8},{1,5},{5,1},{9,13},{13,9},{2,6},{6,2},{1... | collective-permute-start | bytes 6291464 | tf_op jit(solution)/shard_map/ppermute | solution.py:421
  64.3 10.6 %slice-start.2 = ((s8[8388608]{0:T(1024)(128)(4,1)}), s8[4194304]{0:T(1024)(128)(4,1)S(1)}, s32[]{:S(2)}) async-start(s8[8388608]{0:T(1024)(128)(4,1)} %bitcast.72), calls=%async_computation.10 | async-start | bytes 8388608
  70.4 4.5 collective-permute-start.14
  178.0 13.4 %collective-permute-start.20 = (bf16[4,4,64,4096]{3,2,1,0:T(8,128)(2,1)}, bf16[4,4,64,4096]{3,2,1,0:T(8,128)(2,1)S(1)}, u32[]{:S(2)}, u32[]{:S(2)}) collective-permute-start(bf16[4,4,64,4096]{3,2,1,0:T(8,128)(2,1)} %bitcast.79), channel_id=1, source_target_pairs={{0,4},{4,0},{8,12},{12,8},{1,5},{5,1},{9,13},{13,9},{2,6},{6,2},{1... | collective-permute-start | bytes 25165832 | tf_op jit(solution)/shard_map/ppermute | solution.py:421
  178.1 93.3 %collective-permute-start.18 = (bf16[512,32,128]{2,1,0:T(8,128)(2,1)}, bf16[512,32,128]{2,1,0:T(8,128)(2,1)}, u32[]{:S(2)}, u32[]{:S(2)}) collective-permute-start(bf16[512,32,128]{2,1,0:T(8,128)(2,1)} %lend_integrals.6), channel_id=1, source_target_pairs={{0,8},{4,12},{8,0},{12,4},{1,9},{5,13},{9,1},{13,5},{2,10},{6,14},... | collective-permute-start | bytes 12582920 | tf_op jit(solution)/shard_map/ppermute | solution.py:429
  179.6 93.0 %collective-permute-start.19 = (bf16[512,32,128]{2,1,0:T(8,128)(2,1)}, bf16[512,32,128]{2,1,0:T(8,128)(2,1)}, u32[]{:S(2)}, u32[]{:S(2)}) collective-permute-start(bf16[512,32,128]{2,1,0:T(8,128)(2,1)} %lend_integrals.7), channel_id=1, source_target_pairs={{0,16},{16,0},{1,17},{17,1},{2,18},{18,2},{3,19},{19,3},{4,20},{20... | collective-permute-start | bytes 12582920 | tf_op jit(solution)/shard_map/ppermute | solution.py:425
  327.4 62.1 %all-gather.17.cloned.1.call-start = ((), (), s32[]{:S(2)}) async-start(), calls=%async_computation.2 | async-start | bytes 2621440 | tf_op jit(solution)/shard_map/cond/branch_1_fun/all_gather | solution.py:459
  327.4 13.5 %collective-permute-start.3 = (bf16[4,4,64,4096]{3,2,1,0:T(8,128)(2,1)}, bf16[4,4,64,4096]{3,2,1,0:T(8,128)(2,1)}, u32[]{:S(2)}, u32[]{:S(2)}) collective-permute-start(bf16[4,4,64,4096]{3,2,1,0:T(8,128)(2,1)} %get-tuple-element.125.g_ref), channel_id=1, source_target_pairs={{0,4},{4,0},{8,12},{12,8},{1,5},{5,1},{9,13},{13,9},{2,6},{6,2},{1... | collective-permute-start | bytes 25165832 | tf_op jit(solution)/shard_map/cond/branch_1_fun/ppermute | solution.py:421
  389.5 4.4 collective-permute-start.4
  405.8 12.0 %collective-permute-start.21 = (f32[2,2,64,1024]{3,2,1,0:T(8,128)}, f32[2,2,64,1024]{3,2,1,0:T(8,128)S(1)}, u32[]{:S(2)}, u32[]{:S(2)}) collective-permute-start(f32[2,2,64,1024]{3,2,1,0:T(8,128)} %bitcast.39), channel_id=1, source_target_pairs={{0,4},{4,0},{8,12},{12,8},{1,5},{5,1},{9,13},{13,9},{2,6},{6,2},{1... | collective-permute-start | bytes 3145736 | tf_op jit(solution)/shard_map/ppermute | solution.py:421
  418.3 24.9 %collective-permute-start.24 = (f32[2,64,512]{1,2,0:T(8,128)S(1)}, f32[2,64,512]{1,2,0:T(8,128)S(1)}, u32[]{:S(2)}, u32[]{:S(2)}) collective-permute-start(f32[2,64,512]{1,2,0:T(8,128)S(1)} %bitcast.92), channel_id=1, source_target_pairs={{0,8},{4,12},{8,0},{12,4},{1,9},{5,13},{9,1},{13,5},{2,10},{6,14},... | collective-permute-start | bytes 786440 | tf_op jit(solution)/shard_map/ppermute | solution.py:429
  432.1 15.3 %collective-permute-start.22 = (f32[2,64,512]{1,2,0:T(8,128)}, f32[2,64,512]{1,2,0:T(8,128)S(1)}, u32[]{:S(2)}, u32[]{:S(2)}) collective-permute-start(f32[2,64,512]{1,2,0:T(8,128)} %bitcast.41), channel_id=1, source_target_pairs={{0,16},{16,0},{1,17},{17,1},{2,18},{18,2},{3,19},{19,3},{4,20},{20... | collective-permute-start | bytes 786440 | tf_op jit(solution)/shard_map/ppermute | solution.py:425
  443.3 9.4 %collective-permute-start.25 = (f32[64,512]{0,1:T(8,128)S(1)}, f32[64,512]{0,1:T(8,128)S(1)}, u32[]{:S(2)}, u32[]{:S(2)}) collective-permute-start(f32[64,512]{0,1:T(8,128)S(1)} %dynamic-slice_bitcast_fusion), channel_id=1, source_target_pairs={{0,16},{16,0},{1,17},{17,1},{2,18},{18,2},{3,19},{19,3},{4,20},{20... | collective-permute-start | bytes 393224 | tf_op jit(solution)/shard_map/ppermute | solution.py:425
  447.5 7.5 %collective-permute-start.23 = (f32[64,512]{0,1:T(8,128)S(1)}, f32[64,512]{0,1:T(8,128)S(1)}, u32[]{:S(2)}, u32[]{:S(2)}) collective-permute-start(f32[64,512]{0,1:T(8,128)S(1)} %dynamic-slice_bitcast_fusion.1), channel_id=1, source_target_pairs={{0,8},{4,12},{8,0},{12,4},{1,9},{5,13},{9,1},{13,5},{2,10},{6,14},... | collective-permute-start | bytes 393224 | tf_op jit(solution)/shard_map/ppermute | solution.py:429
  (6 other events, 17.9 us)
Sparse Core Ops, SparseCore 0:
  25.7 152.2 all-gather.24
  179.5 147.8 all-gather.26
  329.8 44.1 all-gather.16
